TPU v7x, 32 devices: a whole 2x2x4 slice. The times are simulated.
32 devices in a mesh: rep: 2 (over core), ep: 16 (over z, y, x).
Axes of the slice: x: 2, y: 2, z: 4, core: 2. Of those that a mesh axis runs over, the one named last changes fastest.
Arguments:
- resid_in: bfloat16 [2048, 2048], P(('rep', 'ep')), may hold values from -6 to 6
- context: bfloat16 [2048, 2048], P('rep', 'ep'), may hold values from -6 to 6
- out_proj: bfloat16 [2048, 2048], P('ep'), may hold values from -0.125 to 0.125
- norm_gain: float32 [2048], replicated, may hold values from 0.5 to 1.5
- router: bfloat16 [2048, 64], replicated, may hold values from -0.03125 to 0.03125
- routes: int32 [2048, 8], P(('rep', 'ep')), may hold values from 0 to 63, all different within a row; in each aligned block of 64 rows (0 to 63, 64 to 127, ...) at most 10 rows name the same one
- w_gate: bfloat16 [2048, 65536], P(None, ('rep', 'ep')), may hold values from -0.125 to 0.125
- w_up: bfloat16 [2048, 65536], P(None, ('rep', 'ep')), may hold values from -0.125 to 0.125
- w_down: bfloat16 [65536, 2048], P(('rep', 'ep')), may hold values from -0.5 to 0.5
- next_gain: float32 [2048], replicated, may hold values from 0.5 to 1.5
Outputs:
- resid_out: bfloat16 [2048, 2048], P(('rep', 'ep'))
- next_normed: bfloat16 [2048, 2048], P(('rep', 'ep'))
Inputs may be any that keep to these rules, and one draw needn't show every extreme that they name: `routes`: each row names 8 different experts. Among the 64 rows of one device no expert is named by more than 10 rows, a bound that some block reaches.
All inputs are finite; a program needn't handle non-finite values.
Results may differ from a plain program's by a relative error of at most 0.014.
Values may be sent and summed in bfloat16 or wider, within the bound.
A program may use at most 192 MiB of HBM per device.

v0:
```python
import jax
import jax.numpy as jnp
from jax import lax
from jax.sharding import PartitionSpec as P

FF_E = 1024
MOST = 10


def rms_norm(values, gain_row):
    widened = values.astype(jnp.float32)
    factor = lax.rsqrt(jnp.mean(widened * widened, axis=-1, keepdims=True) + 1e-06)
    return (widened * factor * gain_row).astype(jnp.bfloat16)


def body(resid_in, context, out_proj, norm_gain, router, routes, w_gate, w_up, w_down, next_gain):
    model_width = resid_in.shape[1]
    rep_count = lax.axis_size("rep")
    ep_count = lax.axis_size("ep")
    token_ctx = lax.all_to_all(context, "ep", split_axis=0, concat_axis=1, tiled=True)
    attention = jnp.dot(
        token_ctx,
        lax.all_gather(out_proj, "ep", axis=0, tiled=True),
        preferred_element_type=jnp.float32,
    )
    hidden = (resid_in.astype(jnp.float32) + attention).astype(jnp.bfloat16)
    normed = rms_norm(hidden, norm_gain)
    logits = jnp.dot(normed, router, preferred_element_type=jnp.float32)
    experts = router.shape[1]
    picked_mask = (
        routes[:, :, None] == jnp.arange(experts, dtype=jnp.int32)[None, None, :]
    ).astype(jnp.int32)
    picked = jnp.sum(picked_mask.astype(jnp.float32) * logits[:, None, :], axis=2)
    raised = jnp.exp(picked)
    route_weight = (raised / jnp.sum(raised, axis=1, keepdims=True)).astype(jnp.bfloat16)
    units = w_gate.shape[1]
    owners = max(FF_E // units, 1)
    per_device = max(units // FF_E, 1)
    block_size = min(units, FF_E)
    named_count = jnp.sum(picked_mask, axis=1)
    before = jnp.cumsum(named_count, axis=0) - named_count
    order_rank = jnp.sum(picked_mask * before[:, None, :], axis=2)
    owner_part = jnp.arange(owners, dtype=jnp.int32)
    target = (routes[:, :, None] * owners + owner_part[None, None, :]) // per_device
    local_expert = (routes % per_device)[:, :, None]
    slot_width = per_device * MOST
    slot_index = target * slot_width + local_expert * MOST + order_rank[:, :, None]
    slot_total = rep_count * ep_count * slot_width
    slot_hits = slot_index[None] == jnp.arange(slot_total, dtype=jnp.int32)[:, None, None, None]
    pair_hits = jnp.any(slot_hits, axis=3)
    placing = jnp.any(pair_hits, axis=2).astype(jnp.bfloat16)
    outgoing = jnp.dot(placing, normed, preferred_element_type=jnp.bfloat16)
    outgoing = outgoing.reshape(rep_count, ep_count, slot_width, model_width)
    arrived = lax.all_to_all(
        lax.all_to_all(outgoing, "rep", split_axis=0, concat_axis=0, tiled=True),
        "ep",
        split_axis=1,
        concat_axis=1,
        tiled=True,
    )
    slot_rows = arrived.reshape(rep_count * ep_count, per_device, MOST, model_width)
    gate_local = w_gate.reshape(model_width, per_device, block_size)
    up_local = w_up.reshape(model_width, per_device, block_size)
    down_local = w_down.reshape(per_device, block_size, model_width)
    gate_h = jnp.einsum("spmd,dpf->spmf", slot_rows, gate_local, preferred_element_type=jnp.float32)
    up_h = jnp.einsum("spmd,dpf->spmf", slot_rows, up_local, preferred_element_type=jnp.float32)
    activated = (jax.nn.silu(gate_h) * up_h).astype(jnp.bfloat16)
    produced = jnp.einsum(
        "spmf,pfd->spmd", activated, down_local, preferred_element_type=jnp.float32
    ).astype(jnp.bfloat16)
    produced = produced.reshape(rep_count, ep_count, slot_width, model_width)
    returned = lax.all_to_all(
        lax.all_to_all(produced, "rep", split_axis=0, concat_axis=0, tiled=True),
        "ep",
        split_axis=1,
        concat_axis=1,
        tiled=True,
    )
    returned = returned.reshape(slot_total, model_width)
    weighing = jnp.einsum(
        "stk,tk->ts", pair_hits.astype(jnp.float32), route_weight.astype(jnp.float32)
    ).astype(jnp.bfloat16)
    expert_sum = jnp.dot(weighing, returned, preferred_element_type=jnp.float32)
    resid_out = (hidden.astype(jnp.float32) + expert_sum).astype(jnp.bfloat16)
    next_normed = rms_norm(resid_out, next_gain)
    return (resid_out, next_normed)


def solution(mesh):
    in_specs = (
        P(("rep", "ep"), None),
        P("rep", "ep"),
        P("ep", None),
        P(),
        P(),
        P(("rep", "ep"), None),
        P(None, ("rep", "ep")),
        P(None, ("rep", "ep")),
        P(("rep", "ep"), None),
        P(),
    )
    out_specs = (P(("rep", "ep"), None), P(("rep", "ep"), None))
    return jax.shard_map(body, mesh=mesh, in_specs=in_specs, out_specs=out_specs, check_vma=False)
```

profile of v0, /device:TPU:14, one launch (start us, length us, event | category | flops | bytes accessed | tf_op | source)
XLA Modules:
  0.0 320.7 jit_solution(931428298078411620)
XLA Ops:
  7.2 0.0 copy-start
  7.2 0.0 all-gather.2.cloned.1.call-start
  7.2 0.7 all-gather.2.cloned.1.call-update
  7.9 7.2 %all-to-all-start = ((bf16[16,64,128]{2,1,0:T(8,128)(2,1)}), bf16[16,64,128]{2,1,0:T(8,128)(2,1)S(1)}, u32[]{:S(2)}, u32[]{:S(2)}) async-start(bf16[16,64,128]{2,1,0:T(8,128)(2,1)} %bitcast.67), calls=%async_computation | async-start | bytes 524288 | tf_op jit(solution)/shard_map/all_to_all | solution.py:20
  15.1 0.8 copy.50
  15.8 0.2 convert_reduce_fusion
  16.0 0.1 reduce_window_sum.11
  16.1 1.2 select_reduce_fusion
  17.4 0.5 fusion.15
  17.9 0.2 copy.56
  18.1 0.1 dot_general.29
  18.2 0.0 copy-start.4
  18.2 4.3 %all-to-all-done = bf16[16,64,128]{2,1,0:T(8,128)(2,1)S(1)} async-done(((bf16[16,64,128]{2,1,0:T(8,128)(2,1)}), bf16[16,64,128]{2,1,0:T(8,128)(2,1)S(1)}, u32[]{:S(2)}, u32[]{:S(2)}) %all-to-all-start) | async-done | bytes 262176 | tf_op jit(solution)/shard_map/all_to_all | solution.py:20
  22.5 100.2 %all-gather.2.cloned.1.call-done = bf16[2048,2048]{1,0:T(8,128)(2,1)} async-done(((bf16[128,2048]{1,0:T(8,128)(2,1)}), bf16[2048,2048]{1,0:T(8,128)(2,1)}) %all-gather.2.cloned.1.call-update) | async-done | bytes 8388624 | tf_op jit(solution)/shard_map/all_gather | solution.py:23
  122.7 5.1 %multiply_reduce_fusion = (f32[64]{0:T(128)S(1)}, f32[64,2048]{1,0:T(8,128)S(1)}) fusion(bf16[2048,2048]{1,0:T(8,128)(2,1)} %all-gather.2.cloned.1.call-done, bf16[64,2048]{1,0:T(8,128)(2,1)} %param.10, bf16[16,64,128]{2,1,0:T(8,128)(2,1)S(1)} %all-to-all-done), kind=kOutput, calls=%fused_computation.27 | convolution fusion | flops 537657280 | bytes 9437440 | tf_op jit(solution)/shard_map/dot_general | solution.py:21
  127.7 0.0 copy-start.1
  127.8 0.0 copy-done.4
  127.8 0.9 fusion.21
  128.7 5.8 %all_to_all.39 = bf16[2,16,20,2048]{3,1,2,0:T(8,128)(2,1)S(1)} all-to-all(bf16[2,16,20,2048]{3,1,2,0:T(8,128)(2,1)S(1)} %fusion.21), channel_id=1, replica_groups=mesh['rep'=2,'ep'=16] {'rep'}, dimensions={0} | all-to-all | bytes 5242880 | tf_op jit(solution)/shard_map/all_to_all | solution.py:55
  134.5 4.2 %copy.58 = bf16[2,16,20,2048]{3,0,2,1:T(2,128)(2,1)} copy(bf16[2,16,20,2048]{3,1,2,0:T(8,128)(2,1)S(1)} %all_to_all.39) | data formatting | bytes 5242880 | tf_op jit(solution)/shard_map/all_to_all | solution.py:55
  138.7 6.3 %all-to-all-start.2 = ((bf16[2,16,20,2048]{3,0,2,1:T(2,128)(2,1)}), bf16[2,16,20,2048]{3,0,2,1:T(2,128)(2,1)S(1)}, u32[]{:S(2)}, u32[]{:S(2)}) async-start(bf16[2,16,20,2048]{3,0,2,1:T(2,128)(2,1)} %copy.58), calls=%async_computation.2 | async-start | bytes 5242880 | tf_op jit(solution)/shard_map/all_to_all | solution.py:54
  145.0 14.4 %reshape.87 = bf16[2048,2,1024]{2,1,0:T(2,128)(2,1)} reshape(bf16[2048,2048]{1,0:T(8,128)(2,1)} %param.16) | data formatting | bytes 16777216 | tf_op jit(solution)/shard_map/reshape | solution.py:62
  159.4 14.5 %reshape.88 = bf16[2048,2,1024]{2,1,0:T(2,128)(2,1)} reshape(bf16[2048,2048]{1,0:T(8,128)(2,1)} %param.17) | data formatting | bytes 16777216 | tf_op jit(solution)/shard_map/reshape | solution.py:63
  173.9 31.1 %all-to-all-done.2 = bf16[2,16,20,2048]{3,0,2,1:T(2,128)(2,1)S(1)} async-done(((bf16[2,16,20,2048]{3,0,2,1:T(2,128)(2,1)}), bf16[2,16,20,2048]{3,0,2,1:T(2,128)(2,1)S(1)}, u32[]{:S(2)}, u32[]{:S(2)}) %all-to-all-start.2) | async-done | bytes 2621472 | tf_op jit(solution)/shard_map/all_to_all | solution.py:54
  205.1 1.4 copy.59
  206.5 0.0 copy-start.2
  206.5 9.4 %fusion.2 = f32[2,32,10,1024]{3,1,2,0:T(8,128)} fusion(bf16[32,2,10,2048]{3,0,2,1:T(8,128)(2,1)S(1)} %bitcast.64, bf16[2048,2,1024,1]{2,1,0,3:T(2,128)(2,1)} %bitcast.63), kind=kOutput, calls=%fused_computation.2 | convolution fusion | flops 2684354560 | bytes 13631488 | tf_op jit(solution)/shard_map/spmd,dpf->spmf/dot_general | solution.py:65
  215.9 0.0 copy-done.2
  216.0 13.8 %convolution_convert_fusion = bf16[2,32,10,2048]{3,1,2,0:T(8,128)(2,1)S(1)} fusion(bf16[2,1024,2048,1]{2,1,3,0:T(8,128)(2,1)} %bitcast.68, f32[2,32,10,1024]{3,1,2,0:T(8,128)} %fusion.2, bf16[32,2,10,2048]{3,0,2,1:T(8,128)(2,1)} %bitcast.65, bf16[2048,2,1024,1]{2,1,0,3:T(2,128)(2,1)} %bitcast.62), kind=kOutput, calls=%fused_computation.4 | convolution fusion | flops 5373952000 | bytes 24641536 | tf_op jit(solution)/shard_map/spmf,pfd->spmd/dot_general | solution.py:68
  229.8 0.2 copy.62
  230.0 5.8 %all_to_all.40 = bf16[2,16,20,2048]{3,1,2,0:T(8,128)(2,1)S(1)} all-to-all(bf16[2,16,20,2048]{3,1,2,0:T(8,128)(2,1)S(1)} %copy.62), channel_id=1, replica_groups=mesh['rep'=2,'ep'=16] {'rep'}, dimensions={0} | all-to-all | bytes 5242880 | tf_op jit(solution)/shard_map/all_to_all | solution.py:73
  235.8 4.2 %copy.63 = bf16[2,16,20,2048]{3,0,2,1:T(2,128)(2,1)} copy(bf16[2,16,20,2048]{3,1,2,0:T(8,128)(2,1)S(1)} %all_to_all.40) | data formatting | bytes 5242880 | tf_op jit(solution)/shard_map/all_to_all | solution.py:73
  240.1 5.2 %all-to-all-start.4 = ((bf16[2,16,20,2048]{3,0,2,1:T(2,128)(2,1)}), bf16[2,16,20,2048]{3,0,2,1:T(2,128)(2,1)}, u32[]{:S(2)}, u32[]{:S(2)}) async-start(bf16[2,16,20,2048]{3,0,2,1:T(2,128)(2,1)} %copy.63), calls=%async_computation.4 | async-start | bytes 5242880 | tf_op jit(solution)/shard_map/all_to_all | solution.py:72
  245.2 0.0 copy-done.1
  245.2 0.0 copy-done
  245.2 0.3 fusion.38
  245.5 0.2 fusion.24
  245.8 0.1 copy.55
  245.9 0.1 copy.65
  246.0 1.1 fusion.16
  247.1 58.2 %all-to-all-done.4 = bf16[2,16,20,2048]{3,0,2,1:T(2,128)(2,1)} async-done(((bf16[2,16,20,2048]{3,0,2,1:T(2,128)(2,1)}), bf16[2,16,20,2048]{3,0,2,1:T(2,128)(2,1)}, u32[]{:S(2)}, u32[]{:S(2)}) %all-to-all-start.4) | async-done | bytes 2621472 | tf_op jit(solution)/shard_map/all_to_all | solution.py:72
  305.3 3.0 copy.64
  308.2 2.2 reshape.91
  310.4 2.6 fusion.18
  313.0 0.0 copy-start.3
  313.0 0.0 copy-done.5
  313.1 0.8 fusion.20
  313.9 0.0 copy-done.3
  (7 shorter events, 0.1 us)
Async XLA Ops:
  7.2 238.1 %copy-start = (bf16[2048,64]{0,1:T(8,128)(2,1)S(1)}, bf16[2048,64]{0,1:T(8,128)(2,1)}, u32[]{:S(2)}) copy-start(bf16[2048,64]{0,1:T(8,128)(2,1)} %param.14) | copy-start | bytes 786436
  7.2 115.5 %all-gather.2.cloned.1.call-start = ((), (), s32[]{:S(2)}) async-start(), calls=%async_computation.5 | async-start | bytes 8912896 | tf_op jit(solution)/shard_map/all_gather | solution.py:23
  7.9 14.6 %all-to-all-start = ((bf16[16,64,128]{2,1,0:T(8,128)(2,1)}), bf16[16,64,128]{2,1,0:T(8,128)(2,1)S(1)}, u32[]{:S(2)}, u32[]{:S(2)}) async-start(bf16[16,64,128]{2,1,0:T(8,128)(2,1)} %bitcast.67), calls=%async_computation | async-start | bytes 524288 | tf_op jit(solution)/shard_map/all_to_all | solution.py:20
  18.2 109.6 %copy-start.4 = (f32[2048]{0:T(1024)S(1)}, f32[2048]{0:T(1024)}, u32[]{:S(2)}) copy-start(f32[2048]{0:T(1024)} %param.13) | copy-start | bytes 24580
  127.7 117.5 %copy-start.1 = (f32[64,2048]{1,0:T(8,128)}, f32[64,2048]{1,0:T(8,128)S(1)}, u32[]{:S(2)}) copy-start(f32[64,2048]{1,0:T(8,128)S(1)} %get-tuple-element.3) | copy-start | bytes 1572868
  138.7 66.4 %all-to-all-start.2 = ((bf16[2,16,20,2048]{3,0,2,1:T(2,128)(2,1)}), bf16[2,16,20,2048]{3,0,2,1:T(2,128)(2,1)S(1)}, u32[]{:S(2)}, u32[]{:S(2)}) async-start(bf16[2,16,20,2048]{3,0,2,1:T(2,128)(2,1)} %copy.58), calls=%async_computation.2 | async-start | bytes 5242880 | tf_op jit(solution)/shard_map/all_to_all | solution.py:54
  206.5 9.4 %copy-start.2 = (bf16[2,16,20,2048]{3,1,0,2:T(8,128)(2,1)}, bf16[2,16,20,2048]{3,1,0,2:T(8,128)(2,1)S(1)}, u32[]{:S(2)}) copy-start(bf16[2,16,20,2048]{3,1,0,2:T(8,128)(2,1)S(1)} %copy.59) | copy-start | bytes 7864324
  240.1 65.2 %all-to-all-start.4 = ((bf16[2,16,20,2048]{3,0,2,1:T(2,128)(2,1)}), bf16[2,16,20,2048]{3,0,2,1:T(2,128)(2,1)}, u32[]{:S(2)}, u32[]{:S(2)}) async-start(bf16[2,16,20,2048]{3,0,2,1:T(2,128)(2,1)} %copy.63), calls=%async_computation.4 | async-start | bytes 5242880 | tf_op jit(solution)/shard_map/all_to_all | solution.py:72
  310.4 2.6 copy-start.5
  313.0 0.9 copy-start.3
Sparse Core Ops, SparseCore 0:
  10.8 111.8 all-gather.1
where the time goes:
time: 322 us; the launch traced here: 321 us
  waiting for transfers between devices  194 us (60%)
  local copies, waits for them, and re-layouts  45.4 us (14%)
  matrix products  33.2 us (10%)
  starting transfers between devices  18.7 us (6%)
  between operations  14.2 us (4%)
  blocking collectives  11.7 us (4%)
    all_gather x1, waiting for transfers between devices, body(): lax.all_gather(out_proj, 'ep', axis=0, tiled=True)  100 us
    all_to_all x1, waiting for transfers between devices, body(): lax.all_to_all(lax.all_to_all(produced, 'rep', split_axis=0, concat_axis=...  58.2 us
    all_to_all x1, waiting for transfers between devices, body(): lax.all_to_all(lax.all_to_all(outgoing, 'rep', split_axis=0, concat_axis=...  31.1 us
    reshape x1, local copies, waits for them, and re-layouts, body(): up_local = w_up.reshape(model_width, per_device, block_size)  14.5 us
    reshape x1, local copies, waits for them, and re-layouts, body(): gate_local = w_gate.reshape(model_width, per_device, block_size)  14.4 us
    dot_general x1, matrix products, body(): jnp.einsum('spmf,pfd->spmd', activated, down_local, preferred_element_typ...  13.8 us
    dot_general x1, matrix products, body(): jnp.einsum('spmd,dpf->spmf', slot_rows, gate_local, preferred_element_typ...  9.41 us
    all_to_all x1, starting transfers between devices, body(): lax.all_to_all(context, 'ep', split_axis=0, concat_axis=1, tiled=True)  7.15 us
  transfers between devices with their start and end apart: 4, of which 4 were waited for; matrix products, arithmetic and copies ran while one was open for 11% of the time, Pallas kernels for 0%

commit v1 on v0

--- a/solution.py
+++ b/solution.py
@@ -13,16 +13,45 @@
     return (widened * factor * gain_row).astype(jnp.bfloat16)
 
 
+def project(context, out_proj, rep_count, ep_count):
+    rep_at = lax.axis_index("rep")
+    ep_at = lax.axis_index("ep")
+    columns = out_proj.shape[1] // rep_count
+    swap = [(i, (i + 1) % rep_count) for i in range(rep_count)]
+    rows = context.shape[0] // ep_count
+    blocks = context.reshape(ep_count, rows, context.shape[1])
+    blocks = lax.all_to_all(blocks, "ep", split_axis=0, concat_axis=0, tiled=True)
+    both = jnp.concatenate([blocks, lax.ppermute(blocks, "rep", swap)], axis=1)
+    bits = list(range(ep_count.bit_length() - 1))[::-1]
+    orders = [bits, bits[:-2] + bits[-2:][::-1]]
+    held = lax.dynamic_slice_in_dim(out_proj, rep_at * columns, columns, 1)
+    offsets = [[0], [0]]
+    for step in range(len(bits)):
+        perm = [
+            (r * ep_count + e, r * ep_count + (e ^ (1 << orders[r][step])))
+            for r in range(rep_count)
+            for e in range(ep_count)
+        ]
+        held = jnp.concatenate([held, lax.ppermute(held, ("rep", "ep"), perm)], axis=0)
+        offsets = [o + [v ^ (1 << orders[r][step]) for v in o] for r, o in enumerate(offsets)]
+    places = jnp.bitwise_xor(jnp.array(offsets, jnp.int32)[rep_at], ep_at)
+    ordered = jnp.take(both, places, axis=0)
+    ordered = ordered.transpose(1, 0, 2).reshape(rep_count * rows, -1)
+    product = jnp.dot(ordered, held, preferred_element_type=jnp.float32)
+    mine = product[:rows]
+    theirs = lax.ppermute(product[rows:], "rep", swap)
+    return jnp.where(
+        rep_at == 0,
+        jnp.concatenate([mine, theirs], axis=1),
+        jnp.concatenate([theirs, mine], axis=1),
+    )
+
+
 def body(resid_in, context, out_proj, norm_gain, router, routes, w_gate, w_up, w_down, next_gain):
     model_width = resid_in.shape[1]
     rep_count = lax.axis_size("rep")
     ep_count = lax.axis_size("ep")
-    token_ctx = lax.all_to_all(context, "ep", split_axis=0, concat_axis=1, tiled=True)
-    attention = jnp.dot(
-        token_ctx,
-        lax.all_gather(out_proj, "ep", axis=0, tiled=True),
-        preferred_element_type=jnp.float32,
-    )
+    attention = project(context, out_proj, rep_count, ep_count)
     hidden = (resid_in.astype(jnp.float32) + attention).astype(jnp.bfloat16)
     normed = rms_norm(hidden, norm_gain)
     logits = jnp.dot(normed, router, preferred_element_type=jnp.float32)
@@ -59,15 +88,16 @@
         tiled=True,
     )
     slot_rows = arrived.reshape(rep_count * ep_count, per_device, MOST, model_width)
-    gate_local = w_gate.reshape(model_width, per_device, block_size)
-    up_local = w_up.reshape(model_width, per_device, block_size)
-    down_local = w_down.reshape(per_device, block_size, model_width)
-    gate_h = jnp.einsum("spmd,dpf->spmf", slot_rows, gate_local, preferred_element_type=jnp.float32)
-    up_h = jnp.einsum("spmd,dpf->spmf", slot_rows, up_local, preferred_element_type=jnp.float32)
-    activated = (jax.nn.silu(gate_h) * up_h).astype(jnp.bfloat16)
-    produced = jnp.einsum(
-        "spmf,pfd->spmd", activated, down_local, preferred_element_type=jnp.float32
-    ).astype(jnp.bfloat16)
+    outcomes = []
+    for p in range(per_device):
+        part = slice(p * block_size, (p + 1) * block_size)
+        rows_p = slot_rows[:, p].reshape(-1, model_width)
+        gate_h = jnp.dot(rows_p, w_gate[:, part], preferred_element_type=jnp.float32)
+        up_h = jnp.dot(rows_p, w_up[:, part], preferred_element_type=jnp.float32)
+        activated = (jax.nn.silu(gate_h) * up_h).astype(jnp.bfloat16)
+        made = jnp.dot(activated, w_down[part], preferred_element_type=jnp.float32)
+        outcomes.append(made.astype(jnp.bfloat16).reshape(-1, MOST, model_width))
+    produced = jnp.stack(outcomes, axis=1)
     produced = produced.reshape(rep_count, ep_count, slot_width, model_width)
     returned = lax.all_to_all(
         lax.all_to_all(produced, "rep", split_axis=0, concat_axis=0, tiled=True),

time: 322 us -> 296 us (0.919)
  waiting for transfers between devices: 194 us -> 117 us
  blocking collectives: 11.7 us -> 77.7 us
  between operations: 14.2 us -> 0.93 us
  local copies, waits for them, and re-layouts: 45.4 us -> 38 us
  other arithmetic: 3.1 us -> 7.23 us
    all_gather x1 -> x0, waiting for transfers between devices: 100 us -> none  [body(): lax.all_gather(out_proj, 'ep', axis=0, tiled=True)]
    all_to_all x0 -> x1, blocking collectives: none -> 66 us  [body(): lax.all_to_all(lax.all_to_all(outgoing, 'rep', split_axis=0, concat_axis=...]
    ppermute x0 -> x6, waiting for transfers between devices: none -> 38.2 us  [the longest x4 37.9 us: project(): lax.ppermute(held, ('rep', 'ep'), perm)]
    reshape x2 -> x0, local copies, waits for them, and re-layouts: 28.9 us -> none  [the longest x1 14.5 us: body(): up_local = w_up.reshape(model_width, per_device, block_size)]
    all_to_all x2 -> x1, waiting for transfers between devices: 35.5 us -> 20.2 us  [project(): lax.all_to_all(blocks, 'ep', split_axis=0, concat_axis=0, tiled=True)]
    another operation x0 -> x5, local copies, waits for them, and re-layouts: none -> 10.9 us  [the longest x3 8.25 us: body(): produced = jnp.stack(outcomes, axis=1)]
    ppermute x0 -> x6, starting transfers between devices: none -> 5.7 us  [the longest x4 5.12 us: project(): lax.ppermute(held, ('rep', 'ep'), perm)]
    all_to_all x2 -> x1, starting transfers between devices: 13.5 us -> 7.96 us  [project(): lax.all_to_all(blocks, 'ep', split_axis=0, concat_axis=0, tiled=True)]
  transfers between devices with their start and end apart: 4 -> 8, of which waited for: 4 -> 6; matrix products, arithmetic and copies ran while one was open for 11% -> 3% of each run, Pallas kernels for 0% -> 0%
where the time goes in v1:
time: 296 us; the launch traced here: 295 us
  waiting for transfers between devices  117 us (40%)
  blocking collectives  77.7 us (26%)
  local copies, waits for them, and re-layouts  38 us (13%)
  matrix products  34 us (11%)
  starting transfers between devices  20.1 us (7%)
  other arithmetic  7.23 us (2%)
    all_to_all x1, blocking collectives, body(): lax.all_to_all(lax.all_to_all(outgoing, 'rep', split_axis=0, concat_axis=...  66 us
    all_to_all x1, waiting for transfers between devices, body(): lax.all_to_all(lax.all_to_all(produced, 'rep', split_axis=0, concat_axis=...  58.8 us
    ppermute x4, waiting for transfers between devices, project(): lax.ppermute(held, ('rep', 'ep'), perm)  37.9 us
    all_to_all x1, waiting for transfers between devices, project(): lax.all_to_all(blocks, 'ep', split_axis=0, concat_axis=0, tiled=True)  20.2 us
    dot_general x2, matrix products, body(): made = jnp.dot(activated, w_down[part], preferred_element_type=jnp.float32)  15.8 us
    dot_general x2, matrix products, body(): jnp.dot(rows_p, w_gate[:, part], preferred_element_type=jnp.float32)  10.5 us
    another operation x3, local copies, waits for them, and re-layouts, body(): produced = jnp.stack(outcomes, axis=1)  8.25 us
    all_to_all x1, starting transfers between devices, project(): lax.all_to_all(blocks, 'ep', split_axis=0, concat_axis=0, tiled=True)  7.96 us
  transfers between devices with their start and end apart: 8, of which 6 were waited for; matrix products, arithmetic and copies ran while one was open for 3% of the time, Pallas kernels for 0%

profile of v1, /device:TPU:14, one launch (start us, length us, event | category | flops | bytes accessed | tf_op | source)
XLA Modules:
  0.0 295.2 jit_solution(4521014573356235844)
XLA Ops:
  0.7 1.7 constant_dynamic-update-slice_fusion.4
  2.4 2.6 collective-permute-start.1
  5.0 11.1 %collective-permute-done.1 = bf16[128,1024]{1,0:T(8,128)(2,1)S(1)} collective-permute-done((bf16[128,1024]{1,0:T(8,128)(2,1)S(1)}, bf16[128,1024]{1,0:T(8,128)(2,1)S(1)}, u32[]{:S(2)}, u32[]{:S(2)}) %collective-permute-start.1) | collective-permute-done | bytes 262176 | tf_op jit(solution)/shard_map/ppermute | solution.py:35
  16.1 1.4 collective-permute-start.2
  17.5 12.5 %collective-permute-done.2 = bf16[256,1024]{1,0:T(8,128)(2,1)S(1)} collective-permute-done((bf16[256,1024]{1,0:T(8,128)(2,1)S(1)}, bf16[256,1024]{1,0:T(8,128)(2,1)S(1)}, u32[]{:S(2)}, u32[]{:S(2)}) %collective-permute-start.2) | collective-permute-done | bytes 524320 | tf_op jit(solution)/shard_map/ppermute | solution.py:35
  30.1 0.6 collective-permute-start.3
  30.7 14.3 %collective-permute-done.3 = bf16[512,1024]{1,0:T(8,128)(2,1)S(1)} collective-permute-done((bf16[512,1024]{1,0:T(8,128)(2,1)S(1)}, bf16[512,1024]{1,0:T(8,128)(2,1)S(1)}, u32[]{:S(2)}, u32[]{:S(2)}) %collective-permute-start.3) | collective-permute-done | bytes 1048608 | tf_op jit(solution)/shard_map/ppermute | solution.py:35
  45.0 1.5 pad_maximum_fusion.1
  46.5 0.5 collective-permute-start.4
  47.0 8.0 %all-to-all-start = ((bf16[16,64,128]{2,1,0:T(8,128)(2,1)}), bf16[16,64,128]{2,1,0:T(8,128)(2,1)S(1)}, u32[]{:S(2)}, u32[]{:S(2)}) async-start(bf16[16,64,128]{2,1,0:T(8,128)(2,1)} %bitcast.1), calls=%async_computation | async-start | bytes 524288 | tf_op jit(solution)/shard_map/all_to_all | solution.py:23
  55.3 20.2 %all-to-all-done = bf16[16,64,128]{2,1,0:T(8,128)(2,1)S(1)} async-done(((bf16[16,64,128]{2,1,0:T(8,128)(2,1)}), bf16[16,64,128]{2,1,0:T(8,128)(2,1)S(1)}, u32[]{:S(2)}, u32[]{:S(2)}) %all-to-all-start) | async-done | bytes 262176 | tf_op jit(solution)/shard_map/all_to_all | solution.py:23
  75.6 1.2 select_reduce_fusion
  76.8 0.7 constant_dynamic-update-slice_fusion.3
  77.6 0.6 gather_fusion
  78.7 0.8 constant_dynamic-update-slice_fusion.2
  79.5 1.1 constant_dynamic-update-slice_fusion.1
  80.6 3.1 %constant_dynamic-update-slice_fusion = bf16[2048,1024]{1,0:T(8,128)(2,1)} fusion(bf16[2048,1024]{1,0:T(8,128)(2,1)} %constant_dynamic-update-slice_fusion.1, bf16[1024,1024]{1,0:T(8,128)(2,1)} %collective-permute-done.4), kind=kLoop, calls=%fused_computation.71 | loop fusion | bytes 4194304 | tf_op jit(solution)/shard_map/concatenate | solution.py:35
  83.7 3.0 %fusion.71 = f32[128,1024]{1,0:T(8,128)S(1)} fusion(bf16[128,2048]{0,1:T(8,128)(2,1)S(1)} %bitcast.39, bf16[2048,1024]{1,0:T(8,128)(2,1)} %constant_dynamic-update-slice_fusion), kind=kOutput, calls=%fused_computation.92 | convolution fusion | flops 536870912 | bytes 5242880 | tf_op jit(solution)/shard_map/dot_general | solution.py:40
  86.7 0.6 collective-permute-start.5
  87.3 0.5 fusion.31
  88.1 0.4 collective-permute-done.5
  88.7 0.9 fusion.48
  89.6 5.8 %all_to_all.25 = bf16[2,16,20,2048]{3,1,2,0:T(8,128)(2,1)S(1)} all-to-all(bf16[2,16,20,2048]{3,1,2,0:T(8,128)(2,1)S(1)} %fusion.48), channel_id=1, replica_groups=mesh['rep'=2,'ep'=16] {'rep'}, dimensions={0} | all-to-all | bytes 5242880 | tf_op jit(solution)/shard_map/all_to_all | solution.py:84
  95.4 2.7 copy.68
  98.1 66.0 %all_to_all.26 = bf16[2,16,20,2048]{3,0,2,1:T(2,128)(2,1)S(1)} all-to-all(bf16[2,16,20,2048]{3,0,2,1:T(2,128)(2,1)S(1)} %copy.68), channel_id=1, replica_groups=mesh['rep'=2,'ep'=16] {'ep'}, dimensions={1} | all-to-all | bytes 5242880 | tf_op jit(solution)/shard_map/all_to_all | solution.py:83
  164.2 1.4 copy.69
  165.6 1.3 fusion.69
  166.9 0.8 copy.70
  167.7 1.3 reshape_squeeze.6
  169.0 5.3 %fusion.10 = f32[320,1024]{1,0:T(8,128)} fusion(bf16[320,2048]{1,0:T(8,128)(2,1)} %reshape_squeeze.6, bf16[2048,2048]{1,0:T(8,128)(2,1)} %param.17), kind=kOutput, calls=%fused_computation.12 | convolution fusion | flops 1342177280 | bytes 6815744 | tf_op jit(solution)/shard_map/dot_general | solution.py:95
  174.3 7.9 %fusion.12 = bf16[320,2048]{1,0:T(8,128)(2,1)} fusion(bf16[2048,2048]{1,0:T(8,128)(2,1)} %param.19, bf16[320,2048]{1,0:T(8,128)(2,1)S(1)} %copy-done.3, bf16[2048,2048]{1,0:T(8,128)(2,1)} %param.18, f32[320,1024]{1,0:T(8,128)} %fusion.10), kind=kOutput, calls=%fused_computation.14 | convolution fusion | flops 2686976000 | bytes 12320768 | tf_op jit(solution)/shard_map/dot_general | solution.py:98
  182.2 3.3 %stack_reshape.6 = bf16[32,1,10,2048]{3,2,0,1:T(8,128)(2,1)} reshape(bf16[320,2048]{1,0:T(8,128)(2,1)} %fusion.12) | data formatting | bytes 2621440 | tf_op jit(solution)/shard_map/stack;reshape | solution.py:100
  185.5 2.1 copy.71
  187.6 1.3 reshape_squeeze.7
  188.9 5.3 %fusion.4 = f32[320,1024]{1,0:T(8,128)} fusion(bf16[320,2048]{1,0:T(8,128)(2,1)} %reshape_squeeze.7, bf16[2048,2048]{1,0:T(8,128)(2,1)} %param.17), kind=kOutput, calls=%fused_computation.6 | convolution fusion | flops 1342177280 | bytes 6815744 | tf_op jit(solution)/shard_map/dot_general | solution.py:95
  194.2 7.9 %fusion.15 = bf16[320,2048]{1,0:T(8,128)(2,1)} fusion(bf16[2048,2048]{1,0:T(8,128)(2,1)} %param.19, bf16[320,2048]{1,0:T(8,128)(2,1)S(1)} %copy-done.4, bf16[2048,2048]{1,0:T(8,128)(2,1)} %param.18, f32[320,1024]{1,0:T(8,128)} %fusion.4), kind=kOutput, calls=%fused_computation.15 | convolution fusion | flops 2686976000 | bytes 12320768 | tf_op jit(solution)/shard_map/dot_general | solution.py:98
  202.1 3.5 %stack_reshape.7 = bf16[32,1,10,2048]{3,2,0,1:T(8,128)(2,1)} reshape(bf16[320,2048]{1,0:T(8,128)(2,1)} %fusion.15) | data formatting | bytes 2621440 | tf_op jit(solution)/shard_map/stack;reshape | solution.py:100
  205.6 2.1 pad_maximum_fusion
  207.7 1.4 copy.72
  209.5 5.8 %all_to_all.27 = bf16[2,16,20,2048]{3,1,2,0:T(8,128)(2,1)S(1)} all-to-all(bf16[2,16,20,2048]{3,1,2,0:T(8,128)(2,1)S(1)} %copy.73), channel_id=1, replica_groups=mesh['rep'=2,'ep'=16] {'rep'}, dimensions={0} | all-to-all | bytes 5242880 | tf_op jit(solution)/shard_map/all_to_all | solution.py:103
  215.3 4.2 %copy.74 = bf16[2,16,20,2048]{3,0,2,1:T(2,128)(2,1)} copy(bf16[2,16,20,2048]{3,1,2,0:T(8,128)(2,1)S(1)} %all_to_all.27) | data formatting | bytes 5242880 | tf_op jit(solution)/shard_map/all_to_all | solution.py:103
  219.5 6.4 %all-to-all-start.4 = ((bf16[2,16,20,2048]{3,0,2,1:T(2,128)(2,1)}), bf16[2,16,20,2048]{3,0,2,1:T(2,128)(2,1)}, u32[]{:S(2)}, u32[]{:S(2)}) async-start(bf16[2,16,20,2048]{3,0,2,1:T(2,128)(2,1)} %copy.74), calls=%async_computation.4 | async-start | bytes 5242880 | tf_op jit(solution)/shard_map/all_to_all | solution.py:102
  226.7 1.1 fusion.32
  227.8 58.8 %all-to-all-done.4 = bf16[2,16,20,2048]{3,0,2,1:T(2,128)(2,1)} async-done(((bf16[2,16,20,2048]{3,0,2,1:T(2,128)(2,1)}), bf16[2,16,20,2048]{3,0,2,1:T(2,128)(2,1)}, u32[]{:S(2)}, u32[]{:S(2)}) %all-to-all-start.4) | async-done | bytes 2621472 | tf_op jit(solution)/shard_map/all_to_all | solution.py:102
  286.6 3.0 %copy.75 = bf16[2,16,20,2048]{3,2,1,0:T(8,128)(2,1)S(1)} copy(bf16[2,16,20,2048]{3,0,2,1:T(2,128)(2,1)} %all-to-all-done.4) | data formatting | bytes 5242880 | tf_op jit(solution)/shard_map/all_to_all | solution.py:102
  289.6 2.2 reshape.113
  291.8 2.5 fusion.40
  294.3 0.8 fusion.42
  (51 shorter events, 2.6 us)
Async XLA Ops:
  0.6 225.3 %copy-start = (bf16[2048,64]{0,1:T(8,128)(2,1)S(1)}, bf16[2048,64]{0,1:T(8,128)(2,1)}, u32[]{:S(2)}) copy-start(bf16[2048,64]{0,1:T(8,128)(2,1)} %param.15) | copy-start | bytes 786436
  2.4 13.7 %collective-permute-start.1 = (bf16[128,1024]{1,0:T(8,128)(2,1)S(1)}, bf16[128,1024]{1,0:T(8,128)(2,1)S(1)}, u32[]{:S(2)}, u32[]{:S(2)}) collective-permute-start(bf16[128,1024]{1,0:T(8,128)(2,1)S(1)} %get-tuple-element.5), channel_id=1, source_target_pairs={{0,8},{1,9},{2,10},{3,11},{4,12},{5,13},{6,14},{7,15},{8,0},{9,1},... | collective-permute-start | bytes 786440 | tf_op jit(solution)/shard_map/ppermute | solution.py:35
  16.1 13.9 %collective-permute-start.2 = (bf16[256,1024]{1,0:T(8,128)(2,1)S(1)}, bf16[256,1024]{1,0:T(8,128)(2,1)S(1)}, u32[]{:S(2)}, u32[]{:S(2)}) collective-permute-start(bf16[256,1024]{1,0:T(8,128)(2,1)S(1)} %pad_maximum_fusion.4), channel_id=1, source_target_pairs={{0,4},{1,5},{2,6},{3,7},{4,0},{5,1},{6,2},{7,3},{8,12},{9,13},{10,... | collective-permute-start | bytes 1572872 | tf_op jit(solution)/shard_map/ppermute | solution.py:35
  30.1 24.9 %copy-start.9 = (s32[64,8]{0,1:T(8,128)S(1)}, s32[64,8]{0,1:T(8,128)}, u32[]{:S(2)}) copy-start(s32[64,8]{0,1:T(8,128)} %param.16) | copy-start | bytes 6148
  30.1 25.0 %copy-start.10 = (s32[2,16]{1,0:T(2,128)S(1)}, s32[2,16]{1,0:T(2,128)}, u32[]{:S(2)}) copy-start(s32[2,16]{1,0:T(2,128)} %constant.79.clone) | copy-start | bytes 388
  30.1 14.9 %collective-permute-start.3 = (bf16[512,1024]{1,0:T(8,128)(2,1)S(1)}, bf16[512,1024]{1,0:T(8,128)(2,1)S(1)}, u32[]{:S(2)}, u32[]{:S(2)}) collective-permute-start(bf16[512,1024]{1,0:T(8,128)(2,1)S(1)} %pad_maximum_fusion.2), channel_id=1, source_target_pairs={{0,2},{1,3},{2,0},{3,1},{4,6},{5,7},{6,4},{7,5},{8,10},{9,11},{10,... | collective-permute-start | bytes 3145736 | tf_op jit(solution)/shard_map/ppermute | solution.py:35
  46.5 34.1 %collective-permute-start.4 = (bf16[1024,1024]{1,0:T(8,128)(2,1)}, bf16[1024,1024]{1,0:T(8,128)(2,1)}, u32[]{:S(2)}, u32[]{:S(2)}) collective-permute-start(bf16[1024,1024]{1,0:T(8,128)(2,1)} %pad_maximum_fusion.1), channel_id=1, source_target_pairs={{0,1},{1,0},{2,3},{3,2},{4,5},{5,4},{6,7},{7,6},{8,9},{9,8},{10,11... | collective-permute-start | bytes 6291464 | tf_op jit(solution)/shard_map/ppermute | solution.py:35
  47.0 28.5 %all-to-all-start = ((bf16[16,64,128]{2,1,0:T(8,128)(2,1)}), bf16[16,64,128]{2,1,0:T(8,128)(2,1)S(1)}, u32[]{:S(2)}, u32[]{:S(2)}) async-start(bf16[16,64,128]{2,1,0:T(8,128)(2,1)} %bitcast.1), calls=%async_computation | async-start | bytes 524288 | tf_op jit(solution)/shard_map/all_to_all | solution.py:23
  75.5 2.1 collective-permute-start
  83.7 4.8 %copy-start.6 = (bf16[64,2048]{1,0:T(8,128)(2,1)S(1)}, bf16[64,2048]{1,0:T(8,128)(2,1)}, u32[]{:S(2)}) copy-start(bf16[64,2048]{1,0:T(8,128)(2,1)} %param.11) | copy-start | bytes 786436
  83.7 5.0 %copy-start.7 = (f32[2048]{0:T(1024)S(1)}, f32[2048]{0:T(1024)}, u32[]{:S(2)}) copy-start(f32[2048]{0:T(1024)} %param.14) | copy-start | bytes 24580
  86.7 1.7 collective-permute-start.5
  88.6 137.3 %copy-start.2 = (bf16[64,2048]{1,0:T(8,128)(2,1)}, bf16[64,2048]{1,0:T(8,128)(2,1)S(1)}, u32[]{:S(2)}) copy-start(bf16[64,2048]{1,0:T(8,128)(2,1)S(1)} %get-tuple-element.3) | copy-start | bytes 786436
  169.0 5.3 %copy-start.3 = (bf16[320,2048]{1,0:T(8,128)(2,1)S(1)}, bf16[320,2048]{1,0:T(8,128)(2,1)}, u32[]{:S(2)}) copy-start(bf16[320,2048]{1,0:T(8,128)(2,1)} %reshape_squeeze.6) | copy-start | bytes 3932164
  188.9 5.3 %copy-start.4 = (bf16[320,2048]{1,0:T(8,128)(2,1)S(1)}, bf16[320,2048]{1,0:T(8,128)(2,1)}, u32[]{:S(2)}) copy-start(bf16[320,2048]{1,0:T(8,128)(2,1)} %reshape_squeeze.7) | copy-start | bytes 3932164
  202.1 3.5 %copy-start.1 = (bf16[32,1,10,2048]{3,2,0,1:T(8,128)(2,1)S(1)}, bf16[32,1,10,2048]{3,2,0,1:T(8,128)(2,1)}, u32[]{:S(2)}) copy-start(bf16[32,1,10,2048]{3,2,0,1:T(8,128)(2,1)} %stack_reshape.6) | copy-start | bytes 3932164
  219.5 67.1 %all-to-all-start.4 = ((bf16[2,16,20,2048]{3,0,2,1:T(2,128)(2,1)}), bf16[2,16,20,2048]{3,0,2,1:T(2,128)(2,1)}, u32[]{:S(2)}, u32[]{:S(2)}) async-start(bf16[2,16,20,2048]{3,0,2,1:T(2,128)(2,1)} %copy.74), calls=%async_computation.4 | async-start | bytes 5242880 | tf_op jit(solution)/shard_map/all_to_all | solution.py:102
  291.8 2.5 copy-start.8
  294.3 0.9 copy-start.5
